TPU v7x, 128 devices: a whole 4x4x4 slice. The times are simulated.
128 devices in a mesh: aux: 4 (over y), orb: 32 (over x, z, core).
Axes of the slice: x: 4, y: 4, z: 4, core: 2. Of those that a mesh axis runs over, the one named last changes fastest.
Arguments:
- half_blocks: bfloat16 [8, 32, 128, 2, 128, 128], P('aux', 'orb'), may hold values from -6 to 6
- fit_coeffs: bfloat16 [8, 8], replicated, may hold values from -2 to 2
- pair_map: int32 [32, 128, 2, 2], replicated, may hold values from 0 to 383, as said below
- block_owner: int32 [384, 2], replicated, may hold values from 0 to 127, as said below
- slot_counts: int32 [32, 128], replicated, may hold values from 1 to 2, as said below
Outputs:
- exchange: float32 [2048, 2048], P(('aux', 'orb'))
Inputs may be any that keep to these rules, and one draw needn't show every extreme that they name: pair_map[o, d, s, 0] is a row block below 16; pair_map[o, d, s, 1] is an orbital block owned by device d; pairs may repeat. `block_owner`: every device owns exactly 3 orbital blocks, with local indices 0 to 2. `slot_counts`: some owner device receives 2 live slots from every source orbital index.
All inputs are finite; a program needn't handle non-finite values.
Results may differ from a plain program's by a relative error of at most 0.00051.
Values may be sent and summed in bfloat16 or wider, within the bound.
A program may use at most 128 MiB of HBM per device.

v0:
```python
import math

import jax
import jax.numpy as jnp
from jax import lax
from jax.sharding import PartitionSpec as P

OWNB = 3
NRB = 16


def shards(half_blocks, fit_coeffs, pair_map, block_owner, slot_counts):
    aux_count = lax.axis_size("aux")
    orb_count = lax.axis_size("orb")
    aux_rows = half_blocks.shape[0]
    dev_count = half_blocks.shape[2]
    slot_total = half_blocks.shape[3]
    row_width = half_blocks.shape[4]
    orb_width = half_blocks.shape[5]
    aux_total = fit_coeffs.shape[0]
    owner_index = lax.axis_index("aux") * orb_count + lax.axis_index("orb")
    coeffs = fit_coeffs.reshape(aux_total, aux_count, aux_rows)
    sending = half_blocks.reshape(aux_rows, dev_count, slot_total, row_width, orb_width)
    received = lax.all_to_all(sending, ("aux", "orb"), split_axis=1, concat_axis=0, tiled=True)
    received = received.reshape(aux_count, orb_count, aux_rows, slot_total, row_width, orb_width)
    fitted = jnp.einsum("paq,aoqsxi->posxi", coeffs, received, preferred_element_type=jnp.float32)
    fitted = fitted.astype(jnp.bfloat16)
    counts = lax.dynamic_index_in_dim(slot_counts, owner_index, 1, keepdims=False)
    slot_pairs = lax.dynamic_index_in_dim(pair_map, owner_index, 1, keepdims=False)
    slot_ids = jnp.arange(slot_total, dtype=jnp.int32)
    live_mask = slot_ids[None, :] < counts[:, None]
    local_slot = block_owner[slot_pairs[:, :, 1], 1]
    column = local_slot * NRB + slot_pairs[:, :, 0]
    targets = jnp.arange(OWNB * NRB, dtype=jnp.int32)
    selector = ((column[:, :, None] == targets[None, None, :]) & live_mask[:, :, None]).astype(
        jnp.bfloat16
    )
    gathered = jnp.einsum("osc,posxi->cxpi", selector, fitted, preferred_element_type=jnp.float32)
    stacked = gathered.astype(jnp.bfloat16).reshape(OWNB, NRB * row_width, aux_total * orb_width)
    summed = lax.psum_scatter(
        jnp.einsum("lak,lbk->ab", stacked, stacked, preferred_element_type=jnp.float32),
        ("aux", "orb"),
        scatter_dimension=0,
        tiled=True,
    )
    factor = 1.0 / math.sqrt(block_owner.shape[0] * aux_total * orb_width)
    return summed * factor


def solution(mesh):
    return jax.shard_map(
        shards,
        mesh=mesh,
        in_specs=(P("aux", "orb", None, None, None, None), P(), P(), P(), P()),
        out_specs=P(("aux", "orb"), None),
        check_vma=False,
    )
```

profile of v0, /device:TPU:0, one launch (start us, length us, event | category | flops | bytes accessed | tf_op | source)
XLA Modules:
  0.0 1112.5 jit_solution(711644518647619541)
XLA Ops:
  6.5 0.0 copy-start
  6.5 14.1 %copy.43 = bf16[2,1,128,2,128,128]{5,4,3,0,2,1:T(8,128)(2,1)} copy(bf16[2,1,128,2,128,128]{5,4,3,2,1,0:T(8,128)(2,1)} %param.5) | data formatting | bytes 33554432 | tf_op args[0]
  20.7 0.0 copy-start.2
  20.7 11.7 %all-to-all-start = ((bf16[2,128,2,128,128]{4,3,2,0,1:T(8,128)(2,1)}), bf16[2,128,2,128,128]{4,3,2,0,1:T(8,128)(2,1)}, u32[]{:S(2)}, u32[]{:S(2)}) async-start(bf16[2,128,2,128,128]{4,3,2,0,1:T(8,128)(2,1)} %bitcast.39), calls=%async_computation | async-start | bytes 33554432 | tf_op jit(solution)/shard_map/all_to_all | solution.py:24
  32.3 0.0 copy-start.4
  32.4 0.0 copy-start.3
  32.4 0.0 reduce-scatter.2.cloned.1.call-start
  32.4 0.0 copy-done
  32.4 0.1 constant_dynamic-slice_fusion
  32.6 0.1 copy.25
  32.7 0.1 copy.26
  32.8 0.1 reshape.48
  32.9 0.0 copy-done.2
  32.9 0.9 gather_fusion
  33.8 0.1 mul.28
  33.9 0.1 copy.27
  34.0 0.0 copy-done.4
  34.0 0.1 copy.22
  34.1 0.0 copy-done.3
  34.1 0.2 dynamic-slice_reduce_fusion
  34.3 220.6 %all-to-all-done = bf16[2,128,2,128,128]{4,3,2,0,1:T(8,128)(2,1)} async-done(((bf16[2,128,2,128,128]{4,3,2,0,1:T(8,128)(2,1)}), bf16[2,128,2,128,128]{4,3,2,0,1:T(8,128)(2,1)}, u32[]{:S(2)}, u32[]{:S(2)}) %all-to-all-start) | async-done | bytes 16777248 | tf_op jit(solution)/shard_map/all_to_all | solution.py:24
  255.0 71.1 %bitcast_convert_fusion = bf16[8,32,2,128,128]{4,0,3,2,1:T(8,128)(2,1)} fusion(bf16[8,4,2,1,1,1]{0,2,1,5,4,3:T(2,128)(2,1)S(1)} %bitcast.43, bf16[4,32,2,2,128,128]{5,4,3,2,1,0:T(8,128)(2,1)} %bitcast.6), kind=kOutput, calls=%fused_computation.1 | convolution fusion | flops 142606336 | bytes 33554560 | tf_op jit(solution)/shard_map/paq,aoqsxi->posxi/dot_general | solution.py:26
  326.1 33.1 %fusion.4 = bf16[48,128,8,128]{3,0,1,2:T(8,128)(2,1)} fusion(bf16[8,32,2,128,128]{4,0,3,2,1:T(8,128)(2,1)} %bitcast_convert_fusion, s32[32,2]{0,1:T(2,128)S(1)} %bitcast.42, pred[32,2]{0,1:T(4,128)(4,1)S(1)} %iota_compare_fusion.1), kind=kOutput, calls=%fused_computation.8 | convolution fusion | flops 811603968 | bytes 29360448 | tf_op jit(solution)/shard_map/osc,posxi->cxpi/dot_general | solution.py:38
  359.1 14.4 %copy.29 = bf16[48,128,8,128]{3,2,1,0:T(8,128)(2,1)} copy(bf16[48,128,8,128]{3,0,1,2:T(8,128)(2,1)} %fusion.4) | data formatting | bytes 25165824 | tf_op jit(solution)/shard_map/convert_element_type | solution.py:39
  373.6 19.3 %reshape.47 = bf16[3,2048,1024]{2,1,0:T(8,128)(2,1)} reshape(bf16[48,128,8,128]{3,2,1,0:T(8,128)(2,1)} %copy.29) | data formatting | bytes 25165824 | tf_op jit(solution)/shard_map/reshape | solution.py:39
  392.9 0.0 copy-start.1
  392.9 34.6 %convolution_bitcast_fusion = f32[2048,2048]{1,0:T(8,128)} fusion(bf16[3,2048,1024]{2,1,0:T(8,128)(2,1)} %reshape.47), kind=kOutput, calls=%fused_computation.9 | convolution fusion | flops 25769803776 | bytes 29360128 | tf_op jit(solution)/shard_map/lak,lbk->ab/dot_general | solution.py:41
  427.5 0.0 reduce-scatter.2.cloned.1.call-update
  427.6 676.5 %reduce-scatter.2.cloned.1.call-done = f32[16,2048]{1,0:T(8,128)} async-done(((f32[2048,2048]{1,0:T(8,128)}), f32[16,2048]{1,0:T(8,128)}) %reduce-scatter.2.cloned.1.call-update) | async-done | bytes 131088 | tf_op jit(solution)/shard_map/reduce_scatter | solution.py:40
  1104.0 1.6 broadcast_multiply_fusion
  1105.6 0.0 copy-done.1
  (4 shorter events, 0.0 us)
Async XLA Ops:
  6.5 25.9 %copy-start = (s32[32,128,2,2]{1,3,2,0:T(2,128)S(1)}, s32[32,128,2,2]{1,3,2,0:T(2,128)}, u32[]{:S(2)}) copy-start(s32[32,128,2,2]{1,3,2,0:T(2,128)} %param.7) | copy-start | bytes 196612
  20.7 12.2 %copy-start.2 = (s32[384,2]{0,1:T(2,128)S(1)}, s32[384,2]{0,1:T(2,128)}, u32[]{:S(2)}) copy-start(s32[384,2]{0,1:T(2,128)} %param.8) | copy-start | bytes 9220
  20.7 234.3 %all-to-all-start = ((bf16[2,128,2,128,128]{4,3,2,0,1:T(8,128)(2,1)}), bf16[2,128,2,128,128]{4,3,2,0,1:T(8,128)(2,1)}, u32[]{:S(2)}, u32[]{:S(2)}) async-start(bf16[2,128,2,128,128]{4,3,2,0,1:T(8,128)(2,1)} %bitcast.39), calls=%async_computation | async-start | bytes 33554432 | tf_op jit(solution)/shard_map/all_to_all | solution.py:24
  32.3 1.7 copy-start.4
  32.4 1.7 copy-start.3
  32.4 1071.7 %reduce-scatter.2.cloned.1.call-start = ((), (), s32[]{:S(2)}) async-start(), calls=%async_computation.2 | async-start | bytes 16908288 | tf_op jit(solution)/shard_map/reduce_scatter | solution.py:40
  392.9 712.7 %copy-start.1 = (s32[32,128,2,2]{1,3,2,0:T(2,128)S(1)}, s32[32,128,2,2]{1,3,2,0:T(2,128)}, u32[]{:S(2)}) copy-start(s32[32,128,2,2]{1,3,2,0:T(2,128)} %param.7) | copy-start | bytes 196612
Sparse Core Ops, SparseCore 0:
  427.7 676.3 reduce-scatter.1
where the time goes:
time: 1110 us
  waiting for transfers between devices  897 us (81%)
  matrix products  139 us (13%)
  local copies, waits for them, and re-layouts  49.7 us (4%)
  between operations  13.5 us (1%)
  starting transfers between devices  11.7 us (1%)
    reduce_scatter x1, waiting for transfers between devices, shards(): lax.psum_scatter(jnp.einsum('lak,lbk->ab', stacked, stacked, preferred_el...  676 us
    all_to_all x1, waiting for transfers between devices, shards(): lax.all_to_all(sending, ('aux', 'orb'), split_axis=1, concat_axis=0, tile...  221 us
    dot_general x1, matrix products, shards(): jnp.einsum('paq,aoqsxi->posxi', coeffs, received, preferred_element_type=...  71.1 us
    dot_general x1, matrix products, shards(): jnp.einsum('lak,lbk->ab', stacked, stacked, preferred_element_type=jnp.fl...  34.6 us
    dot_general x1, matrix products, shards(): jnp.einsum('osc,posxi->cxpi', selector, fitted, preferred_element_type=jn...  33.1 us
  transfers between devices with their start and end apart: 2, of which 2 were waited for; matrix products, arithmetic and copies ran while one was open for 0% of the time, Pallas kernels for 0%

commit v1 on v0

v1 whole, which is shorter than its diff:
```python
import functools
import math

import jax
import jax.numpy as jnp
from jax import lax
from jax.experimental import pallas as pl
from jax.experimental.pallas import tpu as pltpu
from jax.sharding import PartitionSpec as P

MESH = pl.DeviceIdType.MESH
OWNB = 3
NRB = 16
MIB = 1 << 20

AXES = ((0, 1, 2), (1, 2, 0), (2, 0, 1))
UNITS = ((0, 0, 0, 80), (1, 0, 80, 96), (2, 0, 176, 80), (0, 1, 0, 96), (1, 1, 96, 80), (2, 1, 176, 80))


def place():
    a, o = lax.axis_index("aux"), lax.axis_index("orb")
    return a, o // 8, (o // 2) % 4, o % 2


def device(y, x, z, c):
    return (y, (x * 4 + z) * 2 + c)


def spread(units, h_ref, out_ref, b1_ref, b2_ref, s1, r1, s2, r2, s3, r3, l1, l3):
    me = place()

    def other(axis, k, dc=0):
        there = list(me)
        there[axis] = (me[axis] + k) % 4
        there[3] = (me[3] + dc) % 2
        return there

    barrier = pltpu.get_barrier_semaphore()
    mates = [other(axis, k, dc) for axis in range(3) for k in (1, 3, 2) for dc in (0, 1)] + [other(0, 0, 1)]
    for there in mates:
        pl.semaphore_signal(barrier, inc=1, device_id=device(*there), device_id_type=MESH)
    pl.semaphore_wait(barrier, len(mates))

    hops = [(1, 0), (3, 0), (2, 0), (1, 1), (3, 1), (2, 1), (0, 1)]

    def ways(u):
        g, q, row, n = units[u]
        return AXES[g] + (q, pl.ds(row, n))

    def at(ref, axes, index, q, rows, core=None):
        where = [slice(None)] * 4
        for axis, value in zip(axes, index):
            where[axis] = value
        if core is not None:
            where[3] = core
        return ref.at[tuple(where) + (q, rows)]

    def taken(axes, index, q, rows, core):
        where = [slice(None)] * 4
        for axis, value in zip(axes, index):
            where[axis] = value
        where[3] = core
        return h_ref.at[(q,) + tuple(where) + (rows,)]

    def remote(src, dst, send, recv, there):
        return pltpu.make_async_remote_copy(src, dst, send, recv, device_id=device(*there), device_id_type=MESH)

    def first_hop(u, j):
        A, B, C, q, rows = ways(u)
        there = other(A, *hops[j])
        return there, s1.at[u, j], r1.at[u, j]

    def start_first(u, j):
        A, B, C, q, rows = ways(u)
        there, send, recv = first_hop(u, j)
        for k in range(4):
            b = (me[B] + k) % 4
            ref = b1_ref if k else b2_ref
            remote(taken((A, B), (there[A], b), q, rows, there[3]), at(ref, (A, B), (me[A], b), q, rows, me[3]), send, recv, there).start()

    def whole_first(u, j):
        A, B, C, q, rows = ways(u)
        there, send, recv = first_hop(u, j)
        return remote(taken((A,), (there[A],), q, rows, there[3]), at(b1_ref, (A,), (me[A],), q, rows, me[3]), send, recv, there)

    def start_own(u):
        A, B, C, q, rows = ways(u)
        for k in range(4):
            b = (me[B] + k) % 4
            ref = b1_ref if k else b2_ref
            pltpu.make_async_copy(taken((A, B), (me[A], b), q, rows, me[3]), at(ref, (A, B), (me[A], b), q, rows, me[3]), l1.at[u]).start()

    def whole_own(u):
        A, B, C, q, rows = ways(u)
        return pltpu.make_async_copy(taken((A,), (me[A],), q, rows, me[3]), at(b1_ref, (A,), (me[A],), q, rows, me[3]), l1.at[u])

    turns = (1, 3, 2)

    def start_second(u, j):
        A, B, C, q, rows = ways(u)
        there = other(B, turns[j])
        for k in range(4):
            c = (me[C] + k) % 4
            ref = b2_ref if k else out_ref
            remote(at(b1_ref, (B, C), (there[B], c), q, rows), at(ref, (B, C), (me[B], c), q, rows), s2.at[u, j], r2.at[u, j], there).start()

    def whole_second(u, j):
        A, B, C, q, rows = ways(u)
        there = other(B, turns[j])
        return remote(at(b1_ref, (B,), (there[B],), q, rows), at(b2_ref, (B,), (me[B],), q, rows), s2.at[u, j], r2.at[u, j], there)

    def kept(u):
        A, B, C, q, rows = ways(u)
        return pltpu.make_async_copy(at(b2_ref, (B, C), (me[B], me[C]), q, rows), at(out_ref, (B, C), (me[B], me[C]), q, rows), l3.at[u])

    def third(u, j):
        A, B, C, q, rows = ways(u)
        there = other(C, turns[j])
        return remote(at(b2_ref, (C,), (there[C],), q, rows), at(out_ref, (C,), (me[C],), q, rows), s3.at[u, j], r3.at[u, j], there)

    n = len(units)
    waves = [list(range(i, min(i + 3, n))) for i in range(0, n, 3)]
    for us in waves:
        for j in range(7):
            for u in us:
                start_first(u, j)
        for u in us:
            start_own(u)
    for us in waves:
        for u in us:
            for j in range(7):
                whole_first(u, j).wait_recv()
            whole_own(u).wait()
        for j in range(3):
            for u in us:
                start_second(u, j)
        for u in us:
            kept(u).start()
    for us in waves:
        for u in us:
            for j in range(3):
                whole_second(u, j).wait_recv()
        for j in range(3):
            for u in us:
                third(u, j).start()
    for us in waves:
        for u in us:
            for j in range(3):
                third(u, j).wait_recv()
            kept(u).wait()
    for u in range(n):
        for j in range(7):
            whole_first(u, j).wait_send()
        for j in range(3):
            whole_second(u, j).wait_send()
            third(u, j).wait_send()


def all_to_all(h, units=UNITS):
    h = h.reshape(2, 4, 4, 4, 2, 256, 128)
    shape = jax.ShapeDtypeStruct((4, 4, 4, 2, 2, 256, 128), jnp.bfloat16)
    n = len(units)
    dma = pltpu.SemaphoreType.DMA
    out, _, _ = pl.pallas_call(
        functools.partial(spread, units),
        out_shape=(shape,) * 3,
        in_specs=[pl.BlockSpec(memory_space=pl.ANY)],
        out_specs=(pl.BlockSpec(memory_space=pl.ANY),) * 3,
        scratch_shapes=[dma((n, 7)), dma((n, 7)), dma((n, 3)), dma((n, 3)), dma((n, 3)), dma((n, 3)), dma((n,)), dma((n,))],
        compiler_params=pltpu.CompilerParams(collective_id=0, has_side_effects=True),
    )(h)
    return out


def fit(column, w_ref, r_ref, g_ref, head, chain, slots, acc, sems):
    target = pl.program_id(0)

    def block(slot):
        return pltpu.make_async_copy(r_ref.at[:, slot // 2, :, slot % 2], slots.at[slot], sems.at[slot])

    @pl.when(target == 0)
    def _():
        def clear(t, _):
            head[t] = -1
            return 0

        def link(slot, _):
            t = column[slot]
            chain[slot] = head[t]
            head[t] = slot
            return 0

        def load(t, _):
            def step(slot):
                block(slot).start()
                return chain[slot]

            lax.while_loop(lambda slot: slot >= 0, step, head[t])
            return 0

        lax.fori_loop(0, OWNB * NRB + 1, clear, 0)
        lax.fori_loop(0, 64, link, 0)
        lax.fori_loop(0, OWNB * NRB, load, 0)

    acc[...] = jnp.zeros_like(acc)

    def add(slot):
        block(slot).wait()
        stack = jnp.concatenate(
            [
                jnp.concatenate([slots[slot, a, q, pl.ds(32 * j, 32), :] for a in range(4) for q in range(2)], axis=0)
                for j in range(4)
            ],
            axis=1,
        )
        acc[...] += jnp.dot(w_ref[...], stack, preferred_element_type=jnp.float32).astype(jnp.bfloat16).astype(jnp.float32)
        return chain[slot]

    lax.while_loop(lambda slot: slot >= 0, add, head[target])
    for p in range(8):
        for j in range(4):
            g_ref[0, pl.ds(32 * j, 32), pl.ds(128 * p, 128)] = acc[pl.ds(32 * p, 32), pl.ds(128 * j, 128)].astype(jnp.bfloat16)


def gather_fit(received, fit_coeffs, pair_map, block_owner, slot_counts):
    owner = lax.axis_index("aux") * 32 + lax.axis_index("orb")
    counts = lax.dynamic_index_in_dim(slot_counts, owner, 1, keepdims=False)
    pairs = lax.dynamic_index_in_dim(pair_map, owner, 1, keepdims=False)
    live = jnp.arange(2, dtype=jnp.int32)[None, :] < counts[:, None]
    column = block_owner[pairs[:, :, 1], 1] * NRB + pairs[:, :, 0]
    column = jnp.where(live, column, OWNB * NRB).reshape(64)
    weights = jnp.kron(fit_coeffs, jnp.eye(32, dtype=jnp.bfloat16))
    smem = pltpu.SMEM
    return pl.pallas_call(
        fit,
        grid=(OWNB * NRB,),
        out_shape=jax.ShapeDtypeStruct((OWNB * NRB, 128, 1024), jnp.bfloat16),
        in_specs=[
            pl.BlockSpec(memory_space=smem),
            pl.BlockSpec((256, 256), lambda t: (0, 0)),
            pl.BlockSpec(memory_space=pl.ANY),
        ],
        out_specs=pl.BlockSpec((1, 128, 1024), lambda t: (t, 0, 0)),
        scratch_shapes=[
            smem((OWNB * NRB + 1,), jnp.int32),
            smem((64,), jnp.int32),
            pltpu.VMEM((64, 4, 2, 128, 128), jnp.bfloat16),
            pltpu.VMEM((256, 512), jnp.float32),
            pltpu.SemaphoreType.DMA((64,)),
        ],
        compiler_params=pltpu.CompilerParams(vmem_limit_bytes=40 * MIB),
    )(column, weights, received)


CUT = ((0, 640), (640, 640), (1280, 768))


def total(factor, g_ref, out_ref, acc, core_out, core_in, held, wire, in1, t2, in2, t3, in3, cs, cr, s1, r1, s2, r2, s3, r3):
    me = place()
    y, x, z, c = me

    def other(axis, k):
        there = list(me)
        there[axis] = (me[axis] + k) % 4
        return device(*there)

    partner = device(y, x, z, 1 - c)
    barrier = pltpu.get_barrier_semaphore()
    mates = [partner] + [other(axis, k) for axis in range(3) for k in (1, 2, 3)]
    for there in mates:
        pl.semaphore_signal(barrier, inc=1, device_id=there, device_id_type=MESH)
    pl.semaphore_wait(barrier, len(mates))

    def remote(src, dst, send, recv, there):
        return pltpu.make_async_remote_copy(src, dst, send, recv, device_id=there, device_id_type=MESH)

    def rows_of(p):
        return (y + 1 + p // 2) % 4, (x // 2 + 1 + p) % 2

    def core_copy(p):
        return remote(core_out.at[p], core_in.at[p], cs.at[p], cr.at[p], partner)

    def form(p):
        ty, pair = rows_of(p)
        first = pl.multiple_of((ty * 4 + pair * 2) * 128, 256)

        @pl.loop(0, 4)
        def _(n):
            start = pl.multiple_of(n * 512, 512)
            part = jnp.zeros((256, 512), jnp.float32)
            for l in range(OWNB):
                part += lax.dot_general(
                    g_ref[l, pl.ds(first, 256), :], g_ref[l, pl.ds(start, 512), :],
                    (((1,), (1,)), ((), ())), preferred_element_type=jnp.float32)
            acc[:, pl.ds(start, 512)] = part

        for j in range(2):
            for k in range(4):
                base = j * 128 + k * 32
                gone = acc[pl.ds(pl.multiple_of(base + 16 * (1 - c), 16), 16), :]
                core_out[p, j, k] = gone.astype(jnp.bfloat16)
        core_copy(p).start()

    def keep(p):
        ty, pair = rows_of(p)
        core_copy(p).wait_recv()
        for j in range(2):
            for k in range(4):
                base = j * 128 + k * 32
                sum_ = acc[pl.ds(pl.multiple_of(base + 16 * c, 16), 16), :] + core_in[p, j, k].astype(jnp.float32)
                held[ty, pair * 2 + j, k] = sum_
                wire[ty, pair * 2 + j, k] = sum_.astype(jnp.bfloat16)
        if p < 6:
            k = p // 2 + 1
            cols = pl.ds(*CUT[0])
            remote(wire.at[ty, pl.ds(pair * 2, 2), :, :, cols], in1[0].at[k - 1, pl.ds(pair * 2, 2)],
                   s1.at[0, k - 1], r1.at[0, k - 1], other(0, k)).start()
        cols = pl.ds(*CUT[1])
        for j in range(2 if p % 2 == 0 else 1):
            tx = pair * 2 + j if p % 2 == 0 else x + 1 - 2 * (x % 2)
            k = (tx - x + 4) % 4
            remote(wire.at[ty, tx, :, :, cols], in1[1].at[k - 1, ty],
                   s1.at[1, k - 1], r1.at[1, k - 1], device(y, tx, z, c)).start()
        cols = pl.ds(*CUT[2])
        for k in (1, 3, 2):
            tz = (z + k) % 4
            remote(wire.at[ty, pl.ds(pair * 2, 2), tz, :, cols], in1[2].at[k - 1, ty, pl.ds(pair * 2, 2)],
                   s1.at[2, k - 1], r1.at[2, k - 1], other(2, k)).start()

    for p in range(8):
        form(p)
        keep(p)

    arrived1 = [remote(in1[g].at[k], in1[g].at[k], s1.at[g, k], r1.at[g, k], partner) for g in range(3) for k in range(3)]
    own1 = (
        lambda i: held[y, i, :, :, pl.ds(*CUT[0])],
        lambda i: held[i, x, :, :, pl.ds(*CUT[1])],
        lambda i: held[i, :, z, :, pl.ds(*CUT[2])],
    )
    go2 = (
        lambda k: (t2[0].at[(x + k) % 4], other(1, k)),
        lambda k: (t2[1].at[:, (z + k) % 4], other(2, k)),
        lambda k: (t2[2].at[(y + k) % 4], other(0, k)),
    )
    copies2 = []
    for g in range(3):
        for k in range(3):
            arrived1[g * 3 + k].wait_recv()
        for i in range(4):
            t2[g][i] = own1[g](i) + (in1[g][0, i].astype(jnp.float32) + in1[g][1, i].astype(jnp.float32)
                                     + in1[g][2, i].astype(jnp.float32))
        for k in (1, 3, 2):
            src, there = go2[g](k)
            copy = remote(src, in2[g].at[k - 1], s2.at[g, k - 1], r2.at[g, k - 1], there)
            copy.start()
            copies2.append(copy)
    own2 = (lambda: t2[0][x], lambda: t2[1][:, z], lambda: t2[2][y])
    go3 = (
        lambda k: (t3[0].at[(z + k) % 4], other(2, k)),
        lambda k: (t3[1].at[(y + k) % 4], other(0, k)),
        lambda k: (t3[2].at[(x + k) % 4], other(1, k)),
    )
    copies3 = []
    for g in range(3):
        for copy in copies2[3 * g:3 * g + 3]:
            copy.wait_recv()
        t3[g][...] = own2[g]() + (in2[g][0] + in2[g][1] + in2[g][2])
        for k in (1, 3, 2):
            src, there = go3[g](k)
            copy = remote(src, in3[g].at[k - 1], s3.at[g, k - 1], r3.at[g, k - 1], there)
            copy.start()
            copies3.append(copy)
    own3 = (lambda: t3[0][z], lambda: t3[1][y], lambda: t3[2][x])
    for g in range(3):
        for copy in copies3[3 * g:3 * g + 3]:
            copy.wait_recv()
        out_ref[:, pl.ds(*CUT[g])] = (own3[g]() + (in3[g][0] + in3[g][1] + in3[g][2])) * factor
    for p in range(8):
        core_copy(p).wait_send()
    for copy in arrived1 + copies2 + copies3:
        copy.wait_send()


def gram_sum(gathered, factor):
    f32, bf16 = jnp.float32, jnp.bfloat16
    dma = pltpu.SemaphoreType.DMA
    width = [n for _, n in CUT]

    def entry(g_ref, out_ref, acc, core_out, core_in, held, wire, *rest):
        bufs, sems = rest[:15], rest[15:]
        total(factor, g_ref, out_ref, acc, core_out, core_in, held, wire,
              bufs[0:3], bufs[3:6], bufs[6:9], bufs[9:12], bufs[12:15], *sems)

    return pl.pallas_call(
        entry,
        out_shape=jax.ShapeDtypeStruct((16, 2048), f32),
        in_specs=[pl.BlockSpec(memory_space=pltpu.VMEM)],
        out_specs=pl.BlockSpec(memory_space=pltpu.VMEM),
        scratch_shapes=[
            pltpu.VMEM((256, 2048), f32),
            pltpu.VMEM((8, 2, 4, 16, 2048), bf16),
            pltpu.VMEM((8, 2, 4, 16, 2048), bf16),
            pltpu.VMEM((4, 4, 4, 16, 2048), f32),
            pltpu.VMEM((4, 4, 4, 16, 2048), bf16),
        ]
        + [pltpu.VMEM((3, 4, 4, 16, n), bf16) for n in width]
        + [pltpu.VMEM((4, 4, 16, n), f32) for n in width]
        + [pltpu.VMEM((3, 4, 16, n), f32) for n in width]
        + [pltpu.VMEM((4, 16, n), f32) for n in width]
        + [pltpu.VMEM((3, 16, n), f32) for n in width]
        + [dma((8,)), dma((8,))] + [dma((3, 3)) for _ in range(6)],
        compiler_params=pltpu.CompilerParams(collective_id=1, has_side_effects=True, vmem_limit_bytes=56 * MIB),
    )(gathered)


def shards(half_blocks, fit_coeffs, pair_map, block_owner, slot_counts):
    received = all_to_all(half_blocks).reshape(4, 32, 2, 2, 128, 128)
    gathered = gather_fit(received, fit_coeffs, pair_map, block_owner, slot_counts)
    factor = 1.0 / math.sqrt(block_owner.shape[0] * fit_coeffs.shape[0] * half_blocks.shape[5])
    return gram_sum(gathered.reshape(OWNB, NRB * 128, 1024), factor)


def solution(mesh):
    return jax.shard_map(
        shards,
        mesh=mesh,
        in_specs=(P("aux", "orb", None, None, None, None), P(), P(), P(), P()),
        out_specs=P(("aux", "orb"), None),
        check_vma=False,
    )
```

time: 1110 us -> 299 us (0.27)
  waiting for transfers between devices: 897 us -> 0 us
  Pallas kernels: 0 us -> 288 us
  matrix products: 139 us -> 0 us
  local copies, waits for them, and re-layouts: 49.7 us -> 9.82 us
  between operations: 13.5 us -> 0.12 us
  starting transfers between devices: 11.7 us -> 0 us
    reduce_scatter x1 -> x0, waiting for transfers between devices: 676 us -> none  [shards(): lax.psum_scatter(jnp.einsum('lak,lbk->ab', stacked, stacked, preferred_el...]
    pallas_call x0 -> x3, Pallas kernels: none -> 288 us  [the longest x1 191 us: all_to_all(): pl.pallas_call(functools.partial(spread, units), out_shape=(shape,) * 3,...]
    all_to_all x1 -> x0, waiting for transfers between devices: 221 us -> none  [shards(): lax.all_to_all(sending, ('aux', 'orb'), split_axis=1, concat_axis=0, tile...]
    dot_general x3 -> x0, matrix products: 139 us -> none  [the longest x1 71.1 us: shards(): jnp.einsum('paq,aoqsxi->posxi', coeffs, received, preferred_element_type=...]
    reshape x1 -> x0, local copies, waits for them, and re-layouts: 19.3 us -> none  [shards(): gathered.astype(jnp.bfloat16)]
    convert_element_type x1 -> x0, local copies, waits for them, and re-layouts: 14.4 us -> none  [shards(): gathered.astype(jnp.bfloat16)]
    all_to_all x1 -> x0, starting transfers between devices: 11.7 us -> none  [shards(): lax.all_to_all(sending, ('aux', 'orb'), split_axis=1, concat_axis=0, tile...]
  transfers between devices with their start and end apart: 2 -> 0, of which waited for: 2 -> 0; matrix products, arithmetic and copies ran while one was open for 0% -> 0% of each run, Pallas kernels for 0% -> 0%
where the time goes in v1:
time: 299 us; the launch traced here: 298 us
  Pallas kernels  288 us (96%)
  local copies, waits for them, and re-layouts  9.82 us (3%)
    pallas_call x1, Pallas kernels, all_to_all(): pl.pallas_call(functools.partial(spread, units), out_shape=(shape,) * 3,...  191 us
    pallas_call x1, Pallas kernels, gram_sum(): pl.pallas_call(entry, out_shape=jax.ShapeDtypeStruct((16, 2048), f32), in...  76.3 us
    pallas_call x1, Pallas kernels, gather_fit(): pl.pallas_call(fit, grid=(OWNB * NRB,), out_shape=jax.ShapeDtypeStruct((O...  20.9 us
    unnamed x11, local copies, waits for them, and re-layouts  6.96 us

profile of v1, /device:TPU:0, one launch (start us, length us, event | category | flops | bytes accessed | tf_op | source)
XLA Modules:
  0.0 298.0 jit_solution(11308505194420510935)
XLA Ops:
  0.0 0.0 copy-start
  0.0 0.0 copy-start.3
  0.0 0.8 copy-done
  0.8 0.1 constant_dynamic-slice_fusion
  1.0 0.1 copy.9
  1.1 0.1 copy.10
  1.2 0.1 reshape.34
  1.3 0.0 copy-start.4
  1.3 1.6 gather_fusion
  2.9 0.1 copy.11
  3.0 0.1 squeeze.11
  3.1 0.0 copy-done.3
  3.1 0.2 dynamic-slice_reduce_fusion
  3.3 0.1 iota_compare_fusion.1
  3.4 0.1 lt.37
  3.5 190.6 %shard_map.55 = (bf16[4,4,4,2,2,256,128]{6,5,4,3,2,1,0:T(8,128)(2,1)}, bf16[4,4,4,2,2,256,128]{6,5,4,3,2,1,0:T(8,128)(2,1)}, bf16[4,4,4,2,2,256,128]{6,5,4,3,2,1,0:T(8,128)(2,1)}) custom-call(bf16[2,4,4,4,2,256,128]{6,5,4,3,2,1,0:T(8,128)(2,1)} %bitcast.11), custom_call_target="tpu_custom_call" | custom-call | tf_op jit(solution)/shard_map/pallas_call | solution.py:164
  194.1 0.0 copy-done.4
  194.1 0.1 broadcast_multiply_fusion
  194.2 0.0 copy-start.1
  194.2 0.4 mul.44.w_ref
  194.6 20.9 %shard_map.56 = bf16[48,128,1024]{2,1,0:T(8,128)(2,1)S(1)} custom-call(s32[64]{0:T(128)S(1)} %fusion.4.column, bf16[256,256]{1,0:T(8,128)(2,1)S(1)} %mul.44.w_ref, bf16[4,32,2,2,128,128]{5,4,3,2,1,0:T(8,128)(2,1)} %bitcast.12), custom_call_target="tpu_custom_call" | custom-call | tf_op jit(solution)/shard_map/pallas_call | solution.py:234
  215.5 0.0 copy-start.2
  215.5 4.5 %copy-done.2 = bf16[48,128,1024]{2,1,0:T(8,128)(2,1)} copy-done((bf16[48,128,1024]{2,1,0:T(8,128)(2,1)}, bf16[48,128,1024]{2,1,0:T(8,128)(2,1)S(1)}, u32[]{:S(2)}) %copy-start.2) | copy-done | bytes 12582936
  220.1 76.3 %shard_map.57 = f32[16,2048]{1,0:T(8,128)} custom-call(bf16[3,2048,1024]{2,1,0:T(8,128)(2,1)} %bitcast.10), custom_call_target="tpu_custom_call" | custom-call | tf_op jit(solution)/shard_map/pallas_call | solution.py:394
  296.4 1.6 copy.13
  298.0 0.0 copy-done.1
  (3 shorter events, 0.0 us)
Async XLA Ops:
  0.0 0.8 copy-start
  0.0 3.1 %copy-start.3 = (s32[32,128]{1,0:T(8,128)S(1)}, s32[32,128]{1,0:T(8,128)}, u32[]{:S(2)}) copy-start(s32[32,128]{1,0:T(8,128)} %param.9) | copy-start | bytes 49156
  1.3 192.8 %copy-start.4 = (bf16[8,8]{1,0:T(8,128)(2,1)S(1)}, bf16[8,8]{1,0:T(8,128)(2,1)}, u32[]{:S(2)}) copy-start(bf16[8,8]{1,0:T(8,128)(2,1)} %param.6) | copy-start | bytes 388
  194.2 103.8 %copy-start.1 = (s32[32,128,2,2]{1,3,2,0:T(2,128)S(1)}, s32[32,128,2,2]{1,3,2,0:T(2,128)}, u32[]{:S(2)}) copy-start(s32[32,128,2,2]{1,3,2,0:T(2,128)} %param.7) | copy-start | bytes 196612
  215.5 4.5 %copy-start.2 = (bf16[48,128,1024]{2,1,0:T(8,128)(2,1)}, bf16[48,128,1024]{2,1,0:T(8,128)(2,1)S(1)}, u32[]{:S(2)}) copy-start(bf16[48,128,1024]{2,1,0:T(8,128)(2,1)S(1)} %shard_map.56) | copy-start | bytes 37748740

commit v2 on v1

v2 whole, which is shorter than its diff:
```python
import functools
import math

import jax
import jax.numpy as jnp
from jax import lax
from jax.experimental import pallas as pl
from jax.experimental.pallas import tpu as pltpu
from jax.sharding import PartitionSpec as P

MESH = pl.DeviceIdType.MESH
OWNB = 3
NRB = 16
MIB = 1 << 20

AXES = ((0, 1, 2), (1, 2, 0), (2, 0, 1))
UNITS = ((0, 0, 0, 80), (1, 0, 80, 96), (2, 0, 176, 80), (0, 1, 0, 96), (1, 1, 96, 80), (2, 1, 176, 80))


def place():
    a, o = lax.axis_index("aux"), lax.axis_index("orb")
    return a, o // 8, (o // 2) % 4, o % 2


def device(y, x, z, c):
    return (y, (x * 4 + z) * 2 + c)


def spread(units, h_ref, pair_ref, local_ref, count_ref, out_ref, column, b1_ref, b2_ref, pairs, local, counts, ts, s1, r1, s2, r2, s3, r3, l1, l3):
    me = place()
    tables = [
        pltpu.make_async_copy(src, dst, ts.at[i])
        for i, (src, dst) in enumerate(((pair_ref, pairs), (local_ref, local), (count_ref, counts)))
    ]
    for copy in tables:
        copy.start()

    def other(axis, k, dc=0):
        there = list(me)
        there[axis] = (me[axis] + k) % 4
        there[3] = (me[3] + dc) % 2
        return there

    barrier = pltpu.get_barrier_semaphore()
    mates = [other(axis, k, dc) for axis in range(3) for k in (1, 3, 2) for dc in (0, 1)] + [other(0, 0, 1)]
    for there in mates:
        pl.semaphore_signal(barrier, inc=1, device_id=device(*there), device_id_type=MESH)
    pl.semaphore_wait(barrier, len(mates))

    hops = [(1, 0), (3, 0), (2, 0), (1, 1), (3, 1), (2, 1), (0, 1)]

    def ways(u):
        g, q, row, n = units[u]
        return AXES[g] + (q, pl.ds(row, n))

    def at(ref, axes, index, q, rows, core=None):
        where = [slice(None)] * 4
        for axis, value in zip(axes, index):
            where[axis] = value
        if core is not None:
            where[3] = core
        return ref.at[tuple(where) + (q, rows)]

    def taken(axes, index, q, rows, core):
        where = [slice(None)] * 4
        for axis, value in zip(axes, index):
            where[axis] = value
        where[3] = core
        return h_ref.at[(q,) + tuple(where) + (rows,)]

    def remote(src, dst, send, recv, there):
        return pltpu.make_async_remote_copy(src, dst, send, recv, device_id=device(*there), device_id_type=MESH)

    def first_hop(u, j):
        A, B, C, q, rows = ways(u)
        there = other(A, *hops[j])
        return there, s1.at[u, j], r1.at[u, j]

    def start_first(u, j):
        A, B, C, q, rows = ways(u)
        there, send, recv = first_hop(u, j)
        for k in range(4):
            b = (me[B] + k) % 4
            ref = b1_ref if k else b2_ref
            remote(taken((A, B), (there[A], b), q, rows, there[3]), at(ref, (A, B), (me[A], b), q, rows, me[3]), send, recv, there).start()

    def whole_first(u, j):
        A, B, C, q, rows = ways(u)
        there, send, recv = first_hop(u, j)
        return remote(taken((A,), (there[A],), q, rows, there[3]), at(b1_ref, (A,), (me[A],), q, rows, me[3]), send, recv, there)

    def start_own(u):
        A, B, C, q, rows = ways(u)
        for k in range(4):
            b = (me[B] + k) % 4
            ref = b1_ref if k else b2_ref
            pltpu.make_async_copy(taken((A, B), (me[A], b), q, rows, me[3]), at(ref, (A, B), (me[A], b), q, rows, me[3]), l1.at[u]).start()

    def whole_own(u):
        A, B, C, q, rows = ways(u)
        return pltpu.make_async_copy(taken((A,), (me[A],), q, rows, me[3]), at(b1_ref, (A,), (me[A],), q, rows, me[3]), l1.at[u])

    turns = (1, 3, 2)

    def start_second(u, j):
        A, B, C, q, rows = ways(u)
        there = other(B, turns[j])
        for k in range(4):
            c = (me[C] + k) % 4
            ref = b2_ref if k else out_ref
            remote(at(b1_ref, (B, C), (there[B], c), q, rows), at(ref, (B, C), (me[B], c), q, rows), s2.at[u, j], r2.at[u, j], there).start()

    def whole_second(u, j):
        A, B, C, q, rows = ways(u)
        there = other(B, turns[j])
        return remote(at(b1_ref, (B,), (there[B],), q, rows), at(b2_ref, (B,), (me[B],), q, rows), s2.at[u, j], r2.at[u, j], there)

    def kept(u):
        A, B, C, q, rows = ways(u)
        return pltpu.make_async_copy(at(b2_ref, (B, C), (me[B], me[C]), q, rows), at(out_ref, (B, C), (me[B], me[C]), q, rows), l3.at[u])

    def third(u, j):
        A, B, C, q, rows = ways(u)
        there = other(C, turns[j])
        return remote(at(b2_ref, (C,), (there[C],), q, rows), at(out_ref, (C,), (me[C],), q, rows), s3.at[u, j], r3.at[u, j], there)

    n = len(units)
    waves = [list(range(i, min(i + 3, n))) for i in range(0, n, 3)]
    for us in waves:
        for j in range(7):
            for u in us:
                start_first(u, j)
        for u in us:
            start_own(u)
    for copy in tables:
        copy.wait()
    owner = (me[0] * 16 + me[1] * 4 + me[2]) * 2 + me[3]

    def target(slot, _):
        o, s = slot // 2, slot % 2
        t = local[1, pairs[o, s, 1, owner]] * NRB + pairs[o, s, 0, owner]
        column[slot] = jnp.where(s < counts[o, owner], t, OWNB * NRB)
        return 0

    lax.fori_loop(0, 64, target, 0)
    for us in waves:
        for u in us:
            for j in range(7):
                whole_first(u, j).wait_recv()
            whole_own(u).wait()
        for j in range(3):
            for u in us:
                start_second(u, j)
        for u in us:
            kept(u).start()
    for us in waves:
        for u in us:
            for j in range(3):
                whole_second(u, j).wait_recv()
        for j in range(3):
            for u in us:
                third(u, j).start()
    for us in waves:
        for u in us:
            for j in range(3):
                third(u, j).wait_recv()
            kept(u).wait()
    for u in range(n):
        for j in range(7):
            whole_first(u, j).wait_send()
        for j in range(3):
            whole_second(u, j).wait_send()
            third(u, j).wait_send()


def all_to_all(h, pair_map, block_owner, slot_counts, units=UNITS):
    h = h.reshape(2, 4, 4, 4, 2, 256, 128)
    pairs, local = jnp.transpose(pair_map, (0, 2, 3, 1)), jnp.transpose(block_owner)
    shape = jax.ShapeDtypeStruct((4, 4, 4, 2, 2, 256, 128), jnp.bfloat16)
    n = len(units)
    dma, smem = pltpu.SemaphoreType.DMA, pltpu.SMEM
    hbm = pl.BlockSpec(memory_space=pltpu.HBM)
    out, column, _, _ = pl.pallas_call(
        functools.partial(spread, units),
        out_shape=(shape, jax.ShapeDtypeStruct((64,), jnp.int32), shape, shape),
        in_specs=[hbm] * 4,
        out_specs=(hbm, pl.BlockSpec(memory_space=smem), hbm, hbm),
        scratch_shapes=[smem(pairs.shape, jnp.int32), smem(local.shape, jnp.int32), smem(slot_counts.shape, jnp.int32), dma((3,)),
                        dma((n, 7)), dma((n, 7)), dma((n, 3)), dma((n, 3)), dma((n, 3)), dma((n, 3)), dma((n,)), dma((n,))],
        compiler_params=pltpu.CompilerParams(collective_id=0, has_side_effects=True),
    )(h, pairs, local, slot_counts)
    return out, column


def fit(column, w_ref, r_ref, out_ref, head, chain, slots, g_ref, acc, sems, gone):
    def block(slot):
        return pltpu.make_async_copy(r_ref.at[:, slot // 2, :, slot % 2], slots.at[slot], sems.at[slot])

    def clear(t, _):
        head[t] = -1
        return 0

    def link(slot, _):
        t = column[slot]
        chain[slot] = head[t]
        head[t] = slot
        return 0

    def load(t, _):
        def begin(slot):
            block(slot).start()
            return chain[slot]

        lax.while_loop(lambda slot: slot >= 0, begin, head[t])
        return 0

    lax.fori_loop(0, OWNB * NRB + 1, clear, 0)
    lax.fori_loop(0, 64, link, 0)
    lax.fori_loop(0, OWNB * NRB, load, 0)

    def fitted(slot, j):
        stack = jnp.concatenate(
            [
                jnp.concatenate([slots[slot, a, q, pl.ds(32 * i, 32), :] for a in range(4) for q in range(2)], axis=0)
                for i in (2 * j, 2 * j + 1)
            ],
            axis=1,
        )
        return jnp.dot(w_ref[...], stack, preferred_element_type=jnp.float32).astype(jnp.bfloat16)

    def place_in(row, col, j, value):
        for p in range(8):
            for i in range(2):
                g_ref[pl.ds(row + 64 * j + 32 * i, 32), pl.ds(pl.multiple_of(col + 128 * p, 128), 128)] = value[32 * p:32 * p + 32, 128 * i:128 * i + 128]

    def pair(target, _):
        row = pl.multiple_of(target % NRB * 128, 128)
        col = pl.multiple_of(target // NRB * 1024, 1024)
        first = head[target]

        @pl.when(first < 0)
        def _():
            g_ref[pl.ds(row, 128), pl.ds(col, 1024)] = jnp.zeros((128, 1024), jnp.bfloat16)

        @pl.when(first >= 0)
        def _():
            block(first).wait()
            second = chain[first]

            @pl.when(second < 0)
            def _():
                for j in range(2):
                    place_in(row, col, j, fitted(first, j))

            @pl.when(second >= 0)
            def _():
                for j in range(2):
                    acc[j] = fitted(first, j).astype(jnp.float32)

                def add(slot):
                    block(slot).wait()
                    for j in range(2):
                        acc[j] += fitted(slot, j).astype(jnp.float32)
                    return chain[slot]

                lax.while_loop(lambda slot: slot >= 0, add, second)
                for j in range(2):
                    place_in(row, col, j, acc[j].astype(jnp.bfloat16))

        there = (pl.ds(row, 128), pl.ds(col, 1024))
        pltpu.make_async_copy(g_ref.at[there], out_ref.at[there], gone).start()
        return 0

    lax.fori_loop(0, OWNB * NRB, pair, 0)
    pltpu.make_async_copy(g_ref, out_ref, gone).wait()


def gather_fit(received, column, fit_coeffs):
    weights = jnp.kron(fit_coeffs, jnp.eye(32, dtype=jnp.bfloat16))
    smem = pltpu.SMEM
    return pl.pallas_call(
        fit,
        out_shape=jax.ShapeDtypeStruct((NRB * 128, OWNB * 1024), jnp.bfloat16),
        in_specs=[
            pl.BlockSpec(memory_space=smem),
            pl.BlockSpec(memory_space=pltpu.VMEM),
            pl.BlockSpec(memory_space=pltpu.HBM),
        ],
        out_specs=pl.BlockSpec(memory_space=pltpu.HBM),
        scratch_shapes=[
            smem((OWNB * NRB + 1,), jnp.int32),
            smem((64,), jnp.int32),
            pltpu.VMEM((64, 4, 2, 128, 128), jnp.bfloat16),
            pltpu.VMEM((NRB * 128, OWNB * 1024), jnp.bfloat16),
            pltpu.VMEM((2, 256, 256), jnp.float32),
            pltpu.SemaphoreType.DMA((64,)),
            pltpu.SemaphoreType.DMA,
        ],
        compiler_params=pltpu.CompilerParams(vmem_limit_bytes=58 * MIB),
    )(column, weights, received)


CUT = ((0, 640), (640, 640), (1280, 768))


def total(factor, g_ref, out_ref, g, acc, core_out, core_in, wire, in1, t2, in2, t3, in3, gs, cs, cr, s1, r1, s2, r2, s3, r3):
    me = place()
    y, x, z, c = me

    def other(axis, k):
        there = list(me)
        there[axis] = (me[axis] + k) % 4
        return device(*there)

    def remote(src, dst, send, recv, there):
        return pltpu.make_async_remote_copy(src, dst, send, recv, device_id=there, device_id_type=MESH)

    def rows_of(p):
        return (y + 1 + p // 2) % 4, (x // 2 + 1 + p) % 2

    def first_row(p):
        ty, pair = rows_of(p)
        return pl.multiple_of((ty * 4 + pair * 2) * 128, 256)

    def load(p):
        return pltpu.make_async_copy(g_ref.at[pl.ds(first_row(p), 256)], g.at[pl.ds(256 * p, 256)], gs.at[p])

    for p in range(8):
        load(p).start()
    partner = device(y, x, z, 1 - c)
    barrier = pltpu.get_barrier_semaphore()
    mates = [partner] + [other(axis, k) for axis in range(3) for k in (1, 2, 3)]
    for there in mates:
        pl.semaphore_signal(barrier, inc=1, device_id=there, device_id_type=MESH)
    pl.semaphore_wait(barrier, len(mates))

    def core_copy(p):
        return remote(core_out.at[p], core_in.at[p], cs.at[p], cr.at[p], partner)

    def form(p):
        here, mine = pl.ds(256 * p, 256), pl.ds(first_row(p), 256)

        def product(q):
            return lax.dot_general(
                g[here, :], g[256 * q:256 * q + 256, :], (((1,), (1,)), ((), ())), preferred_element_type=jnp.float32)

        @pl.when(c >= 0)
        def _():
            for q in range(p, 8):
                if p == 0:
                    load(q).wait()
                part = product(q)
                acc[here, pl.ds(first_row(q), 256)] = part
                if q > p:
                    acc[256 * q:256 * q + 256, mine] = part.T

        for j in range(2):
            for k in range(4):
                row = pl.multiple_of(256 * p + 128 * j + 32 * k + 16 * (1 - c), 16)
                core_out[p, j, k] = acc[pl.ds(row, 16), :].astype(jnp.bfloat16)
        core_copy(p).start()

    def pass_on(p):
        ty, pair = rows_of(p)
        core_copy(p).wait_recv()
        for j in range(2):
            for k in range(4):
                row = pl.multiple_of(256 * p + 128 * j + 32 * k + 16 * c, 16)
                wire[p, j, k] = (acc[pl.ds(row, 16), :] + core_in[p, j, k].astype(jnp.float32)).astype(jnp.bfloat16)
        if p < 6:
            k = p // 2 + 1
            remote(wire.at[p, :, :, :, pl.ds(*CUT[0])], in1[0].at[k - 1, pl.ds(pair * 2, 2)],
                   s1.at[0, k - 1], r1.at[0, k - 1], other(0, k)).start()
        for j in range(2 if p % 2 == 0 else 1):
            tx = pair * 2 + j if p % 2 == 0 else x + 1 - 2 * (x % 2)
            k = (tx - x + 4) % 4
            remote(wire.at[p, tx % 2, :, :, pl.ds(*CUT[1])], in1[1].at[k - 1, ty],
                   s1.at[1, k - 1], r1.at[1, k - 1], device(y, tx, z, c)).start()
        for k in (1, 3, 2):
            remote(wire.at[p, :, (z + k) % 4, :, pl.ds(*CUT[2])], in1[2].at[k - 1, ty, pl.ds(pair * 2, 2)],
                   s1.at[2, k - 1], r1.at[2, k - 1], other(2, k)).start()

    for p in range(8):
        form(p)
        if p:
            pass_on(p - 1)
    pass_on(7)

    def own(ty, tx, tz, cols):
        p = (ty - y + 3) % 4 * 2 + 1 - (tx // 2 + x // 2) % 2
        row = pl.multiple_of(256 * p + 128 * (tx % 2) + 32 * tz + 16 * c, 16)
        return acc[pl.ds(row, 16), pl.ds(*cols)] + core_in[p, tx % 2, tz, :, pl.ds(*cols)].astype(jnp.float32)

    arrived1 = [remote(in1[g].at[k], in1[g].at[k], s1.at[g, k], r1.at[g, k], partner) for g in range(3) for k in range(3)]
    own1 = (lambda i, j: own(y, i, j, CUT[0]), lambda i, j: own(i, x, j, CUT[1]), lambda i, j: own(i, j, z, CUT[2]))
    go2 = (
        lambda k: (t2[0].at[(x + k) % 4], other(1, k)),
        lambda k: (t2[1].at[:, (z + k) % 4], other(2, k)),
        lambda k: (t2[2].at[(y + k) % 4], other(0, k)),
    )
    copies2 = []
    for n in range(3):
        for k in range(3):
            arrived1[n * 3 + k].wait_recv()
        for i in range(4):
            for j in range(4):
                t2[n][i, j] = own1[n](i, j) + (in1[n][0, i, j].astype(jnp.float32) + in1[n][1, i, j].astype(jnp.float32)
                                               + in1[n][2, i, j].astype(jnp.float32))
        for k in (1, 3, 2):
            src, there = go2[n](k)
            copy = remote(src, in2[n].at[k - 1], s2.at[n, k - 1], r2.at[n, k - 1], there)
            copy.start()
            copies2.append(copy)
    own2 = (lambda: t2[0][x], lambda: t2[1][:, z], lambda: t2[2][y])
    go3 = (
        lambda k: (t3[0].at[(z + k) % 4], other(2, k)),
        lambda k: (t3[1].at[(y + k) % 4], other(0, k)),
        lambda k: (t3[2].at[(x + k) % 4], other(1, k)),
    )
    copies3 = []
    for n in range(3):
        for copy in copies2[3 * n:3 * n + 3]:
            copy.wait_recv()
        t3[n][...] = own2[n]() + (in2[n][0] + in2[n][1] + in2[n][2])
        for k in (1, 3, 2):
            src, there = go3[n](k)
            copy = remote(src, in3[n].at[k - 1], s3.at[n, k - 1], r3.at[n, k - 1], there)
            copy.start()
            copies3.append(copy)
    own3 = (lambda: t3[0][z], lambda: t3[1][y], lambda: t3[2][x])
    for n in range(3):
        for copy in copies3[3 * n:3 * n + 3]:
            copy.wait_recv()
        out_ref[:, pl.ds(*CUT[n])] = (own3[n]() + (in3[n][0] + in3[n][1] + in3[n][2])) * factor
    for p in range(8):
        core_copy(p).wait_send()
    for copy in arrived1 + copies2 + copies3:
        copy.wait_send()


def gram_sum(gathered, factor):
    f32, bf16 = jnp.float32, jnp.bfloat16
    dma = pltpu.SemaphoreType.DMA
    width = [n for _, n in CUT]

    def entry(g_ref, out_ref, g, acc, core_out, core_in, wire, *rest):
        bufs, sems = rest[:15], rest[15:]
        total(factor, g_ref, out_ref, g, acc, core_out, core_in, wire,
              bufs[0:3], bufs[3:6], bufs[6:9], bufs[9:12], bufs[12:15], *sems)

    return pl.pallas_call(
        entry,
        out_shape=jax.ShapeDtypeStruct((16, 2048), f32),
        in_specs=[pl.BlockSpec(memory_space=pltpu.HBM)],
        out_specs=pl.BlockSpec(memory_space=pltpu.VMEM),
        scratch_shapes=[
            pltpu.VMEM((2048, 3072), bf16),
            pltpu.VMEM((2048, 2048), f32),
            pltpu.VMEM((8, 2, 4, 16, 2048), bf16),
            pltpu.VMEM((8, 2, 4, 16, 2048), bf16),
            pltpu.VMEM((8, 2, 4, 16, 2048), bf16),
        ]
        + [pltpu.VMEM((3, 4, 4, 16, n), bf16) for n in width]
        + [pltpu.VMEM((4, 4, 16, n), f32) for n in width]
        + [pltpu.VMEM((3, 4, 16, n), f32) for n in width]
        + [pltpu.VMEM((4, 16, n), f32) for n in width]
        + [pltpu.VMEM((3, 16, n), f32) for n in width]
        + [dma((8,)), dma((8,)), dma((8,))] + [dma((3, 3)) for _ in range(6)],
        compiler_params=pltpu.CompilerParams(collective_id=1, has_side_effects=True, vmem_limit_bytes=58 * MIB),
    )(gathered)


def shards(half_blocks, fit_coeffs, pair_map, block_owner, slot_counts):
    received, column = all_to_all(half_blocks, pair_map, block_owner, slot_counts)
    gathered = gather_fit(received.reshape(4, 32, 2, 2, 128, 128), column, fit_coeffs)
    factor = 1.0 / math.sqrt(block_owner.shape[0] * fit_coeffs.shape[0] * half_blocks.shape[5])
    return gram_sum(gathered, factor)


def solution(mesh):
    return jax.shard_map(
        shards,
        mesh=mesh,
        in_specs=(P("aux", "orb", None, None, None, None), P(), P(), P(), P()),
        out_specs=P(("aux", "orb"), None),
        check_vma=False,
    )
```

time: 299 us -> 269 us (0.90)
  Pallas kernels: 288 us -> 265 us
  local copies, waits for them, and re-layouts: 9.82 us -> 2.6 us
    pallas_call x1, Pallas kernels: 76.3 us -> 56.6 us  [gram_sum(): pl.pallas_call(entry, out_shape=jax.ShapeDtypeStruct((16, 2048), f32), in...]
    unnamed x11 -> x3, local copies, waits for them, and re-layouts: 6.96 us -> 1.57 us
where the time goes in v2:
time: 269 us; the launch traced here: 268 us
  Pallas kernels  265 us (99%)
    pallas_call x1, Pallas kernels, all_to_all(): pl.pallas_call(functools.partial(spread, units), out_shape=(shape, jax.Sh...  191 us
    pallas_call x1, Pallas kernels, gram_sum(): pl.pallas_call(entry, out_shape=jax.ShapeDtypeStruct((16, 2048), f32), in...  56.6 us
    pallas_call x1, Pallas kernels, gather_fit(): pl.pallas_call(fit, out_shape=jax.ShapeDtypeStruct((NRB * 128, OWNB * 102...  17.8 us

profile of v2, /device:TPU:0, one launch (start us, length us, event | category | flops | bytes accessed | tf_op | source)
XLA Modules:
  0.0 268.1 jit_solution(9769266660055117685)
XLA Ops:
  0.0 0.0 copy-start
  0.0 191.0 %shard_map.55 = (bf16[4,4,4,2,2,256,128]{6,5,4,3,2,1,0:T(8,128)(2,1)}, s32[64]{0:T(128)}, bf16[4,4,4,2,2,256,128]{6,5,4,3,2,1,0:T(8,128)(2,1)}, bf16[4,4,4,2,2,256,128]{6,5,4,3,2,1,0:T(8,128)(2,1)}) custom-call(bf16[2,4,4,4,2,256,128]{6,5,4,3,2,1,0:T(8,128)(2,1)} %bitcast.6, s32[32,2,2,128]{3,2,1,0:T(2,128)} %bitcast.8, s32[2,384]{1,0:T(2,128)} %bitcast.9, ...), custom_call_target="tpu_custom_call" | custom-call | tf_op jit(solution)/shard_map/pallas_call | solution.py:183
  191.0 0.0 copy-done
  191.0 0.1 broadcast_multiply_fusion
  191.1 1.0 mul.27.w_ref
  192.1 17.8 %shard_map.56.g_ref = bf16[2048,3072]{1,0:T(8,128)(2,1)} custom-call(s32[64]{0:T(128)} %get-tuple-element.7.column, bf16[256,256]{1,0:T(8,128)(2,1)} %mul.27.w_ref, bf16[4,32,2,2,128,128]{5,4,3,2,1,0:T(8,128)(2,1)} %bitcast.7), custom_call_target="tpu_custom_call" | custom-call | tf_op jit(solution)/shard_map/pallas_call | solution.py:281
  209.9 56.6 %shard_map.57 = f32[16,2048]{1,0:T(8,128)} custom-call(bf16[2048,3072]{1,0:T(8,128)(2,1)} %shard_map.56.g_ref), custom_call_target="tpu_custom_call" | custom-call | tf_op jit(solution)/shard_map/pallas_call | solution.py:451
  266.5 1.6 copy.7
  (1 shorter events, 0.0 us)
Async XLA Ops:
  0.0 191.0 %copy-start = (bf16[8,8]{1,0:T(8,128)(2,1)S(1)}, bf16[8,8]{1,0:T(8,128)(2,1)}, u32[]{:S(2)}) copy-start(bf16[8,8]{1,0:T(8,128)(2,1)} %param.6) | copy-start | bytes 388

commit v3 on v2

--- a/solution.py
+++ b/solution.py
@@ -14,7 +14,10 @@
 MIB = 1 << 20
 
 AXES = ((0, 1, 2), (1, 2, 0), (2, 0, 1))
-UNITS = ((0, 0, 0, 80), (1, 0, 80, 96), (2, 0, 176, 80), (0, 1, 0, 96), (1, 1, 96, 80), (2, 1, 176, 80))
+UNITS = (
+    (0, 0, 0, 96), (1, 0, 96, 32), (1, 1, 0, 48), (2, 1, 48, 80),
+    (0, 0, 128, 80), (1, 0, 208, 48), (1, 1, 128, 48), (2, 1, 176, 80),
+)
 
 
 def place():
@@ -26,7 +29,21 @@
     return (y, (x * 4 + z) * 2 + c)
 
 
-def spread(units, h_ref, pair_ref, local_ref, count_ref, out_ref, column, b1_ref, b2_ref, pairs, local, counts, ts, s1, r1, s2, r2, s3, r3, l1, l3):
+def fitted(w_ref, part, j):
+    stack = jnp.concatenate(
+        [jnp.concatenate([part(a, q, pl.ds(32 * i, 32)) for a in range(4) for q in range(2)], axis=0) for i in (2 * j, 2 * j + 1)],
+        axis=1,
+    )
+    return jnp.dot(w_ref[...], stack, preferred_element_type=jnp.float32).astype(jnp.bfloat16)
+
+
+def pieces(j, value):
+    for p in range(8):
+        for i in range(2):
+            yield 64 * j + 32 * i, 128 * p, value[32 * p:32 * p + 32, 128 * i:128 * i + 128]
+
+
+def spread(units, h_ref, c_ref, pair_ref, local_ref, count_ref, out_ref, ready_ref, column, w_ref, b1_ref, b2_ref, pairs, local, counts, raw, ready, ts, fs, s1, r1, s2, r2, s3, r3, l1, l3):
     me = place()
     tables = [
         pltpu.make_async_copy(src, dst, ts.at[i])
@@ -125,7 +142,7 @@
         return remote(at(b2_ref, (C,), (there[C],), q, rows), at(out_ref, (C,), (me[C],), q, rows), s3.at[u, j], r3.at[u, j], there)
 
     n = len(units)
-    waves = [list(range(i, min(i + 3, n))) for i in range(0, n, 3)]
+    waves = [list(range(n // 2)), list(range(n // 2, n))]
     for us in waves:
         for j in range(7):
             for u in us:
@@ -143,6 +160,12 @@
         return 0
 
     lax.fori_loop(0, 64, target, 0)
+
+    wide = (lax.broadcasted_iota(jnp.int32, (256, 8), 0) // 32 == lax.broadcasted_iota(jnp.int32, (256, 8), 1)).astype(jnp.bfloat16)
+    tall = jnp.dot(wide, c_ref[...], preferred_element_type=jnp.float32).astype(jnp.bfloat16)
+    full = lax.dot_general(tall, wide, (((1,), (1,)), ((), ())), preferred_element_type=jnp.float32)
+    row, col = (lax.broadcasted_iota(jnp.int32, (256, 256), i) % 32 for i in range(2))
+    w_ref[...] = jnp.where(row == col, full, 0.0).astype(jnp.bfloat16)
     for us in waves:
         for u in us:
             for j in range(7):
@@ -160,11 +183,27 @@
         for j in range(3):
             for u in us:
                 third(u, j).start()
-    for us in waves:
+    take = pltpu.make_async_copy(out_ref.at[:, :, :, :, :, pl.ds(0, 128)], raw, fs.at[0])
+    give = pltpu.make_async_copy(ready, ready_ref, fs.at[1])
+
+    def fit_first(o, _):
+        for j in range(2):
+            value = fitted(w_ref, lambda a, q, rows: raw[a, o // 8, o // 2 % 4, o % 2, q, rows, :], j)
+            for row, col, piece in pieces(j, value):
+                ready[o, row:row + 32, col:col + 128] = piece
+        return 0
+
+    for i, us in enumerate(waves):
         for u in us:
             for j in range(3):
                 third(u, j).wait_recv()
             kept(u).wait()
+        if i == 0:
+            take.start()
+            take.wait()
+            lax.fori_loop(0, 32, fit_first, 0)
+            give.start()
+    give.wait()
     for u in range(n):
         for j in range(7):
             whole_first(u, j).wait_send()
@@ -173,28 +212,34 @@
             third(u, j).wait_send()
 
 
-def all_to_all(h, pair_map, block_owner, slot_counts, units=UNITS):
+def all_to_all(h, fit_coeffs, pair_map, block_owner, slot_counts, units=UNITS):
     h = h.reshape(2, 4, 4, 4, 2, 256, 128)
     pairs, local = jnp.transpose(pair_map, (0, 2, 3, 1)), jnp.transpose(block_owner)
     shape = jax.ShapeDtypeStruct((4, 4, 4, 2, 2, 256, 128), jnp.bfloat16)
     n = len(units)
     dma, smem = pltpu.SemaphoreType.DMA, pltpu.SMEM
     hbm = pl.BlockSpec(memory_space=pltpu.HBM)
-    out, column, _, _ = pl.pallas_call(
+    out, ready, column, weights, _, _ = pl.pallas_call(
         functools.partial(spread, units),
-        out_shape=(shape, jax.ShapeDtypeStruct((64,), jnp.int32), shape, shape),
-        in_specs=[hbm] * 4,
-        out_specs=(hbm, pl.BlockSpec(memory_space=smem), hbm, hbm),
-        scratch_shapes=[smem(pairs.shape, jnp.int32), smem(local.shape, jnp.int32), smem(slot_counts.shape, jnp.int32), dma((3,)),
+        out_shape=(shape, jax.ShapeDtypeStruct((32, 128, 1024), jnp.bfloat16), jax.ShapeDtypeStruct((64,), jnp.int32),
+                   jax.ShapeDtypeStruct((256, 256), jnp.bfloat16), shape, shape),
+        in_specs=[hbm, pl.BlockSpec(memory_space=pltpu.VMEM), hbm, hbm, hbm],
+        out_specs=(hbm, hbm, pl.BlockSpec(memory_space=smem), pl.BlockSpec(memory_space=pltpu.VMEM), hbm, hbm),
+        scratch_shapes=[smem(pairs.shape, jnp.int32), smem(local.shape, jnp.int32), smem(slot_counts.shape, jnp.int32),
+                        pltpu.VMEM((4, 4, 4, 2, 2, 128, 128), jnp.bfloat16), pltpu.VMEM((32, 128, 1024), jnp.bfloat16),
+                        dma((3,)), dma((2,)),
                         dma((n, 7)), dma((n, 7)), dma((n, 3)), dma((n, 3)), dma((n, 3)), dma((n, 3)), dma((n,)), dma((n,))],
-        compiler_params=pltpu.CompilerParams(collective_id=0, has_side_effects=True),
-    )(h, pairs, local, slot_counts)
-    return out, column
-
-
-def fit(column, w_ref, r_ref, out_ref, head, chain, slots, g_ref, acc, sems, gone):
+        compiler_params=pltpu.CompilerParams(collective_id=0, has_side_effects=True, vmem_limit_bytes=58 * MIB),
+    )(h, fit_coeffs, pairs, local, slot_counts)
+    return out, ready, column, weights
+
+
+def fit(column, w_ref, ready_ref, r_ref, out_ref, head, chain, slots, ready, g_ref, acc, sems, gone):
+    def tile(target):
+        return pl.ds(pl.multiple_of(target % NRB * 128, 128), 128), pl.ds(pl.multiple_of(target // NRB * 1024, 1024), 1024)
+
     def block(slot):
-        return pltpu.make_async_copy(r_ref.at[:, slot // 2, :, slot % 2], slots.at[slot], sems.at[slot])
+        return pltpu.make_async_copy(r_ref.at[:, slot // 2, :, 1], slots.at[slot // 2], sems.at[slot])
 
     def clear(t, _):
         head[t] = -1
@@ -207,76 +252,89 @@
         return 0
 
     def load(t, _):
+        sole = jnp.logical_and(head[t] >= 0, chain[jnp.maximum(head[t], 0)] < 0)
+
         def begin(slot):
-            block(slot).start()
+            first = slot % 2 == 0
+
+            @pl.when(jnp.logical_and(first, sole))
+            def _():
+                pltpu.make_async_copy(ready_ref.at[slot // 2], g_ref.at[tile(t)], sems.at[slot]).start()
+
+            @pl.when(jnp.logical_and(first, jnp.logical_not(sole)))
+            def _():
+                pltpu.make_async_copy(ready_ref.at[slot // 2], ready.at[slot // 2], sems.at[slot]).start()
+
             return chain[slot]
 
         lax.while_loop(lambda slot: slot >= 0, begin, head[t])
         return 0
 
+    def early(o, _):
+        @pl.when(column[2 * o + 1] < OWNB * NRB)
+        def _():
+            block(2 * o + 1).start()
+
+        return 0
+
+    lax.fori_loop(0, 32, early, 0)
     lax.fori_loop(0, OWNB * NRB + 1, clear, 0)
     lax.fori_loop(0, 64, link, 0)
     lax.fori_loop(0, OWNB * NRB, load, 0)
 
-    def fitted(slot, j):
-        stack = jnp.concatenate(
-            [
-                jnp.concatenate([slots[slot, a, q, pl.ds(32 * i, 32), :] for a in range(4) for q in range(2)], axis=0)
-                for i in (2 * j, 2 * j + 1)
-            ],
-            axis=1,
-        )
-        return jnp.dot(w_ref[...], stack, preferred_element_type=jnp.float32).astype(jnp.bfloat16)
-
-    def place_in(row, col, j, value):
-        for p in range(8):
-            for i in range(2):
-                g_ref[pl.ds(row + 64 * j + 32 * i, 32), pl.ds(pl.multiple_of(col + 128 * p, 128), 128)] = value[32 * p:32 * p + 32, 128 * i:128 * i + 128]
+    def late(slot, j):
+        return fitted(w_ref, lambda a, q, rows: slots[slot // 2, a, q, rows, :], j)
 
     def pair(target, _):
         row = pl.multiple_of(target % NRB * 128, 128)
         col = pl.multiple_of(target // NRB * 1024, 1024)
         first = head[target]
+        second = chain[jnp.maximum(first, 0)]
 
         @pl.when(first < 0)
         def _():
-            g_ref[pl.ds(row, 128), pl.ds(col, 1024)] = jnp.zeros((128, 1024), jnp.bfloat16)
-
-        @pl.when(first >= 0)
+            g_ref[tile(target)] = jnp.zeros((128, 1024), jnp.bfloat16)
+
+        @pl.when(jnp.logical_and(first >= 0, second < 0))
         def _():
             block(first).wait()
-            second = chain[first]
-
-            @pl.when(second < 0)
+
+            @pl.when(first % 2 == 1)
             def _():
                 for j in range(2):
-                    place_in(row, col, j, fitted(first, j))
-
-            @pl.when(second >= 0)
-            def _():
-                for j in range(2):
-                    acc[j] = fitted(first, j).astype(jnp.float32)
-
-                def add(slot):
-                    block(slot).wait()
+                    for r, k, piece in pieces(j, late(first, j)):
+                        g_ref[pl.ds(row + r, 32), pl.ds(pl.multiple_of(col + k, 128), 128)] = piece
+
+        @pl.when(jnp.logical_and(first >= 0, second >= 0))
+        def _():
+            acc[...] = jnp.zeros_like(acc)
+
+            def add(slot):
+                block(slot).wait()
+
+                @pl.when(slot % 2 == 0)
+                def _():
+                    acc[...] += ready[slot // 2].astype(jnp.float32)
+
+                @pl.when(slot % 2 == 1)
+                def _():
                     for j in range(2):
-                        acc[j] += fitted(slot, j).astype(jnp.float32)
-                    return chain[slot]
-
-                lax.while_loop(lambda slot: slot >= 0, add, second)
-                for j in range(2):
-                    place_in(row, col, j, acc[j].astype(jnp.bfloat16))
-
-        there = (pl.ds(row, 128), pl.ds(col, 1024))
-        pltpu.make_async_copy(g_ref.at[there], out_ref.at[there], gone).start()
+                        for r, k, piece in pieces(j, late(slot, j)):
+                            acc[r:r + 32, k:k + 128] += piece.astype(jnp.float32)
+
+                return chain[slot]
+
+            lax.while_loop(lambda slot: slot >= 0, add, first)
+            g_ref[tile(target)] = acc[...].astype(jnp.bfloat16)
+
+        pltpu.make_async_copy(g_ref.at[tile(target)], out_ref.at[tile(target)], gone).start()
         return 0
 
     lax.fori_loop(0, OWNB * NRB, pair, 0)
     pltpu.make_async_copy(g_ref, out_ref, gone).wait()
 
 
-def gather_fit(received, column, fit_coeffs):
-    weights = jnp.kron(fit_coeffs, jnp.eye(32, dtype=jnp.bfloat16))
+def gather_fit(received, ready, column, weights):
     smem = pltpu.SMEM
     return pl.pallas_call(
         fit,
@@ -285,19 +343,21 @@
             pl.BlockSpec(memory_space=smem),
             pl.BlockSpec(memory_space=pltpu.VMEM),
             pl.BlockSpec(memory_space=pltpu.HBM),
+            pl.BlockSpec(memory_space=pltpu.HBM),
         ],
         out_specs=pl.BlockSpec(memory_space=pltpu.HBM),
         scratch_shapes=[
             smem((OWNB * NRB + 1,), jnp.int32),
             smem((64,), jnp.int32),
-            pltpu.VMEM((64, 4, 2, 128, 128), jnp.bfloat16),
+            pltpu.VMEM((32, 4, 2, 128, 128), jnp.bfloat16),
+            pltpu.VMEM((32, 128, 1024), jnp.bfloat16),
             pltpu.VMEM((NRB * 128, OWNB * 1024), jnp.bfloat16),
-            pltpu.VMEM((2, 256, 256), jnp.float32),
+            pltpu.VMEM((128, 1024), jnp.float32),
             pltpu.SemaphoreType.DMA((64,)),
             pltpu.SemaphoreType.DMA,
         ],
         compiler_params=pltpu.CompilerParams(vmem_limit_bytes=58 * MIB),
-    )(column, weights, received)
+    )(column, weights, ready, received)
 
 
 CUT = ((0, 640), (640, 640), (1280, 768))
@@ -471,8 +531,8 @@
 
 
 def shards(half_blocks, fit_coeffs, pair_map, block_owner, slot_counts):
-    received, column = all_to_all(half_blocks, pair_map, block_owner, slot_counts)
-    gathered = gather_fit(received.reshape(4, 32, 2, 2, 128, 128), column, fit_coeffs)
+    received, ready, column, weights = all_to_all(half_blocks, fit_coeffs, pair_map, block_owner, slot_counts)
+    gathered = gather_fit(received.reshape(4, 32, 2, 2, 128, 128), ready, column, weights)
     factor = 1.0 / math.sqrt(block_owner.shape[0] * fit_coeffs.shape[0] * half_blocks.shape[5])
     return gram_sum(gathered, factor)
 

time: 269 us -> 265 us (0.985)
    pallas_call x1, Pallas kernels: 17.8 us -> 12.8 us  [gather_fit(): pl.pallas_call(fit, out_shape=jax.ShapeDtypeStruct((NRB * 128, OWNB * 102...]
where the time goes in v3:
time: 265 us
  Pallas kernels  263 us (99%)
    pallas_call x1, Pallas kernels, all_to_all(): pl.pallas_call(functools.partial(spread, units), out_shape=(shape, jax.Sh...  192 us
    pallas_call x1, Pallas kernels, gram_sum(): pl.pallas_call(entry, out_shape=jax.ShapeDtypeStruct((16, 2048), f32), in...  58 us
    pallas_call x1, Pallas kernels, gather_fit(): pl.pallas_call(fit, out_shape=jax.ShapeDtypeStruct((NRB * 128, OWNB * 102...  12.8 us

profile of v3, /device:TPU:0, one launch (start us, length us, event | category | flops | bytes accessed | tf_op | source)
XLA Modules:
  0.0 264.7 jit_solution(4113508096031307981)
XLA Ops:
  0.0 192.3 %shard_map.55 = (bf16[4,4,4,2,2,256,128]{6,5,4,3,2,1,0:T(8,128)(2,1)}, bf16[32,128,1024]{2,1,0:T(8,128)(2,1)}, s32[64]{0:T(128)}, bf16[256,256]{1,0:T(8,128)(2,1...) custom-call(bf16[2,4,4,4,2,256,128]{6,5,4,3,2,1,0:T(8,128)(2,1)} %bitcast.5, ...), custom_call_target="tpu_custom_call" | custom-call | tf_op jit(solution)/shard_map/pallas_call | solution.py:222
  192.3 12.8 %shard_map.56.g_ref = bf16[2048,3072]{1,0:T(8,128)(2,1)} custom-call(s32[64]{0:T(128)} %get-tuple-element.9.column, bf16[256,256]{1,0:T(8,128)(2,1)} %get-tuple-element.10.w_ref, bf16[32,128,1024]{2,1,0:T(8,128)(2,1)} %get-tuple-element.11.ready_ref, bf16[4,32,2,2,128,128]{5,4,3,2,1,0:T(8,128)(2,1)} %bitcast.4), custom_call_target="tpu_custom_call" | custom-call | tf_op jit(solution)/shard_map/pallas_call | solution.py:339
  205.1 58.0 %shard_map.57 = f32[16,2048]{1,0:T(8,128)} custom-call(bf16[2048,3072]{1,0:T(8,128)(2,1)} %shard_map.56.g_ref), custom_call_target="tpu_custom_call" | custom-call | tf_op jit(solution)/shard_map/pallas_call | solution.py:511
  263.1 1.6 copy.7

commit v4 on v3

--- a/solution.py
+++ b/solution.py
@@ -307,7 +307,17 @@
 
         @pl.when(jnp.logical_and(first >= 0, second >= 0))
         def _():
-            acc[...] = jnp.zeros_like(acc)
+            block(first).wait()
+
+            @pl.when(first % 2 == 0)
+            def _():
+                acc[...] = ready[first // 2].astype(jnp.float32)
+
+            @pl.when(first % 2 == 1)
+            def _():
+                for j in range(2):
+                    for r, k, piece in pieces(j, late(first, j)):
+                        acc[r:r + 32, k:k + 128] = piece.astype(jnp.float32)
 
             def add(slot):
                 block(slot).wait()
@@ -324,7 +334,7 @@
 
                 return chain[slot]
 
-            lax.while_loop(lambda slot: slot >= 0, add, first)
+            lax.while_loop(lambda slot: slot >= 0, add, second)
             g_ref[tile(target)] = acc[...].astype(jnp.bfloat16)
 
         pltpu.make_async_copy(g_ref.at[tile(target)], out_ref.at[tile(target)], gone).start()

time: 265 us -> 264 us (level)
  no operation moved by 1% of the time
where the time goes in v4:
time: 264 us; the launch traced here: 263 us
  Pallas kernels  262 us (99%)
    pallas_call x1, Pallas kernels, all_to_all(): pl.pallas_call(functools.partial(spread, units), out_shape=(shape, jax.Sh...  192 us
    pallas_call x1, Pallas kernels, gram_sum(): pl.pallas_call(entry, out_shape=jax.ShapeDtypeStruct((16, 2048), f32), in...  56.5 us
    pallas_call x1, Pallas kernels, gather_fit(): pl.pallas_call(fit, out_shape=jax.ShapeDtypeStruct((NRB * 128, OWNB * 102...  12.7 us

profile of v4, /device:TPU:0, one launch (start us, length us, event | category | flops | bytes accessed | tf_op | source)
XLA Modules:
  0.0 263.1 jit_solution(14935801264213049979)
XLA Ops:
  0.0 192.3 %shard_map.55 = (bf16[4,4,4,2,2,256,128]{6,5,4,3,2,1,0:T(8,128)(2,1)}, bf16[32,128,1024]{2,1,0:T(8,128)(2,1)}, s32[64]{0:T(128)}, bf16[256,256]{1,0:T(8,128)(2,1...) custom-call(bf16[2,4,4,4,2,256,128]{6,5,4,3,2,1,0:T(8,128)(2,1)} %bitcast.5, ...), custom_call_target="tpu_custom_call" | custom-call | tf_op jit(solution)/shard_map/pallas_call | solution.py:222
  192.3 12.7 %shard_map.56.g_ref = bf16[2048,3072]{1,0:T(8,128)(2,1)} custom-call(s32[64]{0:T(128)} %get-tuple-element.9.column, bf16[256,256]{1,0:T(8,128)(2,1)} %get-tuple-element.10.w_ref, bf16[32,128,1024]{2,1,0:T(8,128)(2,1)} %get-tuple-element.11.ready_ref, bf16[4,32,2,2,128,128]{5,4,3,2,1,0:T(8,128)(2,1)} %bitcast.4), custom_call_target="tpu_custom_call" | custom-call | tf_op jit(solution)/shard_map/pallas_call | solution.py:349
  205.0 56.5 %shard_map.57 = f32[16,2048]{1,0:T(8,128)} custom-call(bf16[2048,3072]{1,0:T(8,128)(2,1)} %shard_map.56.g_ref), custom_call_target="tpu_custom_call" | custom-call | tf_op jit(solution)/shard_map/pallas_call | solution.py:521
  261.6 1.6 copy.7
